TPU v7x, 128 devices: a whole 4x4x4 slice. The times are simulated.
128 devices in a mesh: row: 16 (over z_hi, y, core), col: 8 (over z_lo, x).
Axes of the slice: x: 4, y: 4, z: 4 (z_hi: 2, z_lo: 2; z = z_hi * 2 + z_lo), core: 2. Of those that a mesh axis runs over, the one named last changes fastest.
Arguments:
- token_ids: int32 [16384], P(('row', 'col')), may hold values from 0 to 511
- embedding: bfloat16 [512, 8192], replicated, may hold values from -6 to 6
- norm_gain: bfloat16 [8192], replicated, may hold values from 0.099609375 to 1.8984375
- w_in: bfloat16 [8192, 12288], P(None, ('row', 'col')), may hold values from -0.0625 to 0.0625
- short_taps: float32 [7, 12288], replicated, may hold values from -2 to 2
- long_filter: float32 [16384, 4096], P(('row', 'col')), may hold values from -0.046875 to 0.046875
- skip_gain: float32 [4096], replicated, may hold values from -1 to 1
Outputs:
- mixed_out: bfloat16 [16384, 4096], P(('row', 'col'))
All inputs are finite; a program needn't handle non-finite values.
Results may differ from a plain program's by a relative error of at most 0.0095.
Values may be sent and summed in bfloat16 or wider, within the bound.
No kernel may reach another device: no remote copies, remote signals or barrier semaphores. Data moves between devices by JAX's collectives and lax.ppermute only.
A program may use at most 192 MiB of HBM per device.

v0:
```python
import math
import jax
import jax.numpy as jnp
from jax import lax
from jax.sharding import PartitionSpec as P

FFT_COLS = 128
EPSILON = 1e-05


def passed_along(x, axis, by):
    length = lax.axis_size(axis)
    pairs = [(i, i + by) for i in range(length) if 0 <= i + by < length]
    return lax.ppermute(x, axis, pairs)


def phase_table(first_index, second_index, period):
    turns = first_index * second_index % period
    return 2.0 * math.pi / period * turns.astype(jnp.float32)


def contract(form, table_part, data_part):
    return jnp.einsum(form, table_part, data_part, precision=lax.Precision.HIGHEST)


def project_table(embedding, norm_gain, w_in):
    rows_f32 = embedding.astype(jnp.float32)
    inverse_rms = lax.rsqrt(jnp.mean(rows_f32 * rows_f32, axis=1, keepdims=True) + EPSILON)
    normed = (rows_f32 * inverse_rms * norm_gain.astype(jnp.float32)).astype(jnp.bfloat16)
    own_columns = jnp.dot(normed, w_in, preferred_element_type=jnp.float32).astype(jnp.bfloat16)
    return lax.all_gather(own_columns, ("row", "col"), axis=1, tiled=True)


def short_filter(mixed_rows, short_taps):
    tap_count = short_taps.shape[0]
    row_count = mixed_rows.shape[0]
    earlier = passed_along(mixed_rows[row_count - (tap_count - 1) :], ("row", "col"), 1)
    extended = jnp.concatenate([earlier, mixed_rows], axis=0).astype(jnp.float32)
    result = short_taps[0] * extended[tap_count - 1 :]
    for offset in range(1, tap_count):
        begin_at = tap_count - 1 - offset
        result = result + short_taps[offset] * extended[begin_at : begin_at + row_count]
    return result


def local_causal(signal_all, filter_all):
    seq_len = signal_all.shape[0]
    width = signal_all.shape[1]
    short_len = seq_len // FFT_COLS
    first_len = 2 * short_len
    total_len = first_len * FFT_COLS
    angle_one = phase_table(
        lax.iota(jnp.int32, short_len)[:, None], lax.iota(jnp.int32, first_len)[None, :], first_len
    )
    cos_one = jnp.cos(angle_one)
    sin_one = jnp.sin(angle_one)
    angle_twist = phase_table(
        lax.iota(jnp.int32, first_len)[:, None], lax.iota(jnp.int32, FFT_COLS)[None, :], total_len
    )
    cos_twist = jnp.cos(angle_twist)
    sin_twist = jnp.sin(angle_twist)
    angle_two = phase_table(
        lax.iota(jnp.int32, FFT_COLS)[:, None], lax.iota(jnp.int32, FFT_COLS)[None, :], FFT_COLS
    )
    cos_two = jnp.cos(angle_two)
    sin_two = jnp.sin(angle_two)

    def forward(series):
        blocked = series.reshape(short_len, FFT_COLS, width)
        real_part = contract("sk,sjc->ckj", cos_one, blocked)
        imag_part = -contract("sk,sjc->ckj", sin_one, blocked)
        turned_re = real_part * cos_twist + imag_part * sin_twist
        turned_im = imag_part * cos_twist - real_part * sin_twist
        out_re = contract("jm,ckj->ckm", cos_two, turned_re) + contract(
            "jm,ckj->ckm", sin_two, turned_im
        )
        out_im = contract("jm,ckj->ckm", cos_two, turned_im) - contract(
            "jm,ckj->ckm", sin_two, turned_re
        )
        return (out_re, out_im)

    signal_re, signal_im = forward(signal_all)
    filter_re, filter_im = forward(filter_all)
    product_re = signal_re * filter_re - signal_im * filter_im
    product_im = signal_re * filter_im + signal_im * filter_re
    back_re = contract("jm,ckm->ckj", cos_two, product_re) - contract(
        "jm,ckm->ckj", sin_two, product_im
    )
    back_im = contract("jm,ckm->ckj", cos_two, product_im) + contract(
        "jm,ckm->ckj", sin_two, product_re
    )
    turned_re = back_re * cos_twist - back_im * sin_twist
    turned_im = back_im * cos_twist + back_re * sin_twist
    summed = contract("sk,ckj->sjc", cos_one, turned_re) - contract(
        "sk,ckj->sjc", sin_one, turned_im
    )
    return (summed * (1.0 / total_len)).reshape(seq_len, width)


def local(token_ids, embedding, norm_gain, w_in, short_taps, long_filter, skip_gain):
    lookup_table = project_table(embedding, norm_gain, w_in)
    vocab_size = lookup_table.shape[0]
    one_hot = (token_ids[:, None] == lax.iota(jnp.int32, vocab_size)[None, :]).astype(jnp.bfloat16)
    mixed_rows = jnp.dot(one_hot, lookup_table, preferred_element_type=jnp.float32).astype(
        jnp.bfloat16
    )
    filtered = short_filter(mixed_rows, short_taps)
    channels = filtered.shape[1] // 3
    gate_out = filtered[:, :channels]
    signal = filtered[:, channels : 2 * channels] * filtered[:, 2 * channels :]
    signal_all, filter_all = (
        lax.all_to_all(signal, ("row", "col"), split_axis=1, concat_axis=0, tiled=True),
        lax.all_to_all(long_filter, ("row", "col"), split_axis=1, concat_axis=0, tiled=True),
    )
    causal_all = local_causal(signal_all, filter_all)
    long_part = lax.all_to_all(causal_all, ("row", "col"), split_axis=0, concat_axis=1, tiled=True)
    mixed_out = gate_out * (long_part + skip_gain * signal)
    return mixed_out.astype(jnp.bfloat16)


def solution(mesh):
    in_specs = (
        P(("row", "col")),
        P(),
        P(),
        P(None, ("row", "col")),
        P(),
        P(("row", "col"), None),
        P(),
    )
    out_specs = P(("row", "col"), None)
    return jax.shard_map(local, mesh=mesh, in_specs=in_specs, out_specs=out_specs, check_vma=False)
```

profile of v0, /device:TPU:0, one launch (start us, length us, event | category | flops | bytes accessed | tf_op | source)
XLA Modules:
  0.0 561.6 jit_solution(3965734877258306150)
XLA Ops:
  6.5 5.3 fusion
  12.8 3.7 fusion.54
  19.5 11.7 %all-to-all-start.1 = ((f32[128,128,32]{0,2,1:T(8,128)}), f32[128,128,32]{0,2,1:T(8,128)}, u32[]{:S(2)}, u32[]{:S(2)}) async-start(f32[128,128,32]{0,2,1:T(8,128)} %bitcast.114), calls=%async_computation.1 | async-start | bytes 4194304 | tf_op jit(solution)/shard_map/all_to_all | solution.py:113
  32.2 30.5 %all-to-all-done.1 = f32[128,128,32]{0,2,1:T(8,128)} async-done(((f32[128,128,32]{0,2,1:T(8,128)}), f32[128,128,32]{0,2,1:T(8,128)}, u32[]{:S(2)}, u32[]{:S(2)}) %all-to-all-start.1) | async-done | bytes 2097184 | tf_op jit(solution)/shard_map/all_to_all | solution.py:113
  62.7 9.3 %fusion.38 = f32[256,128,32]{1,0,2:T(8,128)} fusion(f32[128,128,32]{0,2,1:T(8,128)} %all-to-all-done.1), kind=kOutput, calls=%fused_computation.58 | convolution fusion | flops 1611071488 | bytes 6291456 | tf_op jit(solution)/shard_map/sk,sjc->ckj/dot_general | solution.py:23
  71.9 281.6 %all-gather.2.cloned.1.call-done = bf16[512,12288]{0,1:T(8,128)(2,1)} async-done(((bf16[512,96]{0,1:T(8,128)(2,1)}), bf16[512,12288]{0,1:T(8,128)(2,1)}) %all-gather.2.cloned.1.call-update) | async-done | bytes 12582928 | tf_op jit(solution)/shard_map/all_gather | solution.py:31
  353.6 8.8 %convolution_convert_fusion = bf16[128,12288]{1,0:T(8,128)(2,1)S(1)} fusion(bf16[512,12288]{0,1:T(8,128)(2,1)} %all-gather.2.cloned.1.call-done, s32[128]{0:T(128)S(1)} %copy-done.10), kind=kOutput, calls=%fused_computation.5 | convolution fusion | flops 1612251136 | bytes 15729152 | tf_op jit(solution)/shard_map/dot_general | solution.py:104
  362.4 3.9 collective-permute-start
  366.3 9.3 %fusion.40 = f32[256,128,32]{1,0,2:T(8,128)} fusion(f32[128,128,32]{0,2,1:T(8,128)} %all-to-all-done.1), kind=kOutput, calls=%fused_computation.60 | convolution fusion | flops 1611071488 | bytes 6291456 | tf_op jit(solution)/shard_map/sk,sjc->ckj/dot_general | solution.py:23
  376.5 5.2 fusion.7
  388.8 11.1 %all-to-all-start = ((f32[128,128,32]{0,2,1:T(8,128)}), f32[128,128,32]{0,2,1:T(8,128)}, u32[]{:S(2)}, u32[]{:S(2)}) async-start(f32[128,128,32]{0,2,1:T(8,128)} %bitcast.115), calls=%async_computation | async-start | bytes 4194304 | tf_op jit(solution)/shard_map/all_to_all | solution.py:112
  399.9 6.8 %fusion.13 = f32[32,256,128]{2,1,0:T(8,128)S(1)} fusion(f32[256,128,32]{1,0,2:T(8,128)} %fusion.40, f32[256,128,32]{1,0,2:T(8,128)} %fusion.38, f32[256,128]{1,0:T(8,128)S(1)} %copy.49, f32[256,128]{1,0:T(8,128)S(1)} %copy.47), kind=kOutput, calls=%fused_computation.22 | convolution fusion | flops 1615036416 | bytes 12845056 | tf_op jit(solution)/shard_map/jm,ckj->ckm/dot_general | solution.py:23
  406.7 4.2 fusion.15
  410.9 5.8 %fusion.34 = f32[32,256,128]{2,1,0:T(8,128)} fusion(f32[32,256,128]{2,1,0:T(8,128)S(1)} %fusion.13, f32[256,128,32]{1,0,2:T(8,128)S(1)} %copy-done.3, f32[256,128,32]{1,0,2:T(8,128)S(1)} %copy-done.2, f32[256,128]{1,0:T(8,128)S(1)} %copy.49, f32[256,128]{1,0:T(8,128)S(1)} %copy.47), kind=kOutput, calls=%fused_computation.50 | convolution fusion | flops 1616084992 | bytes 17039360 | tf_op jit(solution)/shard_map/jm,ckj->ckm/dot_general | solution.py:23
  416.7 5.8 %fusion.31 = f32[32,256,128]{2,1,0:T(8,128)} fusion(f32[32,256,128]{2,1,0:T(8,128)S(1)} %fusion.15, f32[256,128,32]{1,0,2:T(8,128)S(1)} %copy-done.3, f32[256,128,32]{1,0,2:T(8,128)S(1)} %copy-done.2, f32[256,128]{1,0:T(8,128)S(1)} %copy.49, f32[256,128]{1,0:T(8,128)S(1)} %copy.47), kind=kOutput, calls=%fused_computation.49 | convolution fusion | flops 1616084992 | bytes 17039360 | tf_op jit(solution)/shard_map/jm,ckj->ckm/dot_general | solution.py:23
  422.5 6.8 %all-to-all-done = f32[128,128,32]{0,2,1:T(8,128)} async-done(((f32[128,128,32]{0,2,1:T(8,128)}), f32[128,128,32]{0,2,1:T(8,128)}, u32[]{:S(2)}, u32[]{:S(2)}) %all-to-all-start) | async-done | bytes 2097184 | tf_op jit(solution)/shard_map/all_to_all | solution.py:112
  429.3 3.1 copy.41
  432.5 5.7 %fusion.42 = f32[128,32,256]{2,0,1:T(8,128)S(1)} fusion(f32[128,128,32]{1,0,2:T(8,128)} %copy.41), kind=kOutput, calls=%fused_computation.62 | convolution fusion | flops 1611071488 | bytes 6291456 | tf_op jit(solution)/shard_map/sk,sjc->ckj/dot_general | solution.py:23
  438.2 4.0 fusion.44
  442.2 9.4 %fusion.57 = f32[32,256,128]{2,1,0:T(8,128)} fusion(f32[128,32,256]{2,0,1:T(8,128)S(1)} %fusion.44, f32[128,32,256]{2,0,1:T(8,128)S(1)} %fusion.42, f32[256,128]{0,1:T(8,128)S(1)} %get-tuple-element.14, f32[256,128]{0,1:T(8,128)S(1)} %get-tuple-element.15), kind=kOutput, calls=%fused_computation.74 | convolution fusion | flops 1615036416 | bytes 12845056 | tf_op jit(solution)/shard_map/jm,ckj->ckm/dot_general | solution.py:23
  451.6 7.4 %fusion.61 = f32[32,256,128]{2,1,0:T(8,128)S(1)} fusion(f32[128,32,256]{2,0,1:T(8,128)S(1)} %fusion.44, f32[128,32,256]{2,0,1:T(8,128)S(1)} %fusion.42, f32[256,128]{0,1:T(8,128)S(1)} %get-tuple-element.14, f32[256,128]{0,1:T(8,128)S(1)} %get-tuple-element.15), kind=kOutput, calls=%fused_computation.75 | convolution fusion | flops 1615036416 | bytes 12845056 | tf_op jit(solution)/shard_map/jm,ckj->ckm/dot_general | solution.py:23
  459.0 9.1 %convolution_add_fusion.1 = f32[32,256,128]{2,1,0:T(8,128)} fusion(f32[32,256,128]{2,1,0:T(8,128)S(1)} %fusion.61, f32[128,32,256]{2,0,1:T(8,128)S(1)} %fusion.44, f32[128,32,256]{2,0,1:T(8,128)S(1)} %fusion.42, f32[256,128]{0,1:T(8,128)S(1)} %get-tuple-element.14, f32[256,128]{0,1:T(8,128)S(1)} %get-tuple-element.15), kind=kOutput, calls=%fused_computation.54 | convolution fusion | flops 1616084992 | bytes 17039360 | tf_op jit(solution)/shard_map/jm,ckj->ckm/dot_general | solution.py:23
  468.1 11.9 %multiply_add_fusion = (f32[32,256,128]{2,1,0:T(8,128)S(1)}, f32[32,256,128]{2,1,0:T(8,128)S(1)}) fusion(f32[32,256,128]{2,1,0:T(8,128)} %fusion.31, f32[32,256,128]{2,1,0:T(8,128)} %convolution_add_fusion.1, f32[32,256,128]{2,1,0:T(8,128)} %fusion.34, f32[32,256,128]{2,1,0:T(8,128)} %fusion.57, f32[128,32,256]{2,0,1:T(8,128)S(1)} %fusion.44, ...), kind=kOutput, calls=%fused_computation.44 | convolution fusion | flops 1622376448 | bytes 33816576 | tf_op jit(solution)/shard_map/jm,ckj->ckm/dot_general | solution.py:23
  480.1 4.2 fusion.91
  484.2 4.2 fusion.93
  488.4 4.9 convolution_add_fusion
  493.3 4.2 convolution_subtract_fusion
  497.6 4.2 fusion.23
  501.7 5.8 %multiply_bitcast_fusion = f32[128,128,32]{0,1,2:T(8,128)} fusion(f32[32,128,128]{2,1,0:T(8,128)S(1)} %fusion.23, f32[32,256,128]{1,2,0:T(8,128)S(1)} %convolution_add_fusion, f32[32,256,128]{1,2,0:T(8,128)S(1)} %convolution_subtract_fusion, f32[256,128]{0,1:T(8,128)S(1)} %get-tuple-element.14, f32[256,128]{0,1:T(8,128)S(1)} %get-tuple-element.15), kind=kOutput, calls=%fused_computation.66 | convolution fusion | flops 1615265792 | bytes 12845056 | tf_op jit(solution)/shard_map/sk,ckj->sjc/dot_general | solution.py:23
  507.5 3.1 copy.56
  510.7 35.6 %all_to_all.48 = f32[128,128,32]{1,2,0:T(8,128)} all-to-all(f32[128,128,32]{1,2,0:T(8,128)} %copy.56), channel_id=1, replica_groups=mesh['row'=16,'col'=8] {'row','col'}, dimensions={0} | all-to-all | bytes 4194304 | tf_op jit(solution)/shard_map/all_to_all | solution.py:116
  549.2 5.0 fusion.37
  (37 shorter events, 16.0 us)
Async XLA Ops:
  6.5 5.3 copy-start
  6.5 5.3 copy-start.9
  6.5 347.0 %all-gather.2.cloned.1.call-start = ((), (), s32[]{:S(2)}) async-start(), calls=%async_computation.3 | async-start | bytes 12681216 | tf_op jit(solution)/shard_map/all_gather | solution.py:31
  6.5 6.3 %copy-start.6 = (bf16[512,8192]{1,0:T(8,128)(2,1)S(1)}, bf16[512,8192]{1,0:T(8,128)(2,1)}, u32[]{:S(2)}) copy-start(bf16[512,8192]{1,0:T(8,128)(2,1)} %param.8) | copy-start | bytes 25165828
  16.5 15.4 %copy-start.7 = (f32[7,12288]{1,0:T(8,128)S(1)}, f32[7,12288]{1,0:T(8,128)}, u32[]{:S(2)}) copy-start(f32[7,12288]{1,0:T(8,128)} %param.11) | copy-start | bytes 1032196
  19.5 43.2 %all-to-all-start.1 = ((f32[128,128,32]{0,2,1:T(8,128)}), f32[128,128,32]{0,2,1:T(8,128)}, u32[]{:S(2)}, u32[]{:S(2)}) async-start(f32[128,128,32]{0,2,1:T(8,128)} %bitcast.114), calls=%async_computation.1 | async-start | bytes 4194304 | tf_op jit(solution)/shard_map/all_to_all | solution.py:113
  31.2 322.4 %copy-start.10 = (s32[128]{0:T(128)S(1)}, s32[128]{0:T(128)}, u32[]{:S(2)}) copy-start(s32[128]{0:T(128)} %param.7) | copy-start | bytes 1540
  362.4 13.2 %collective-permute-start = (bf16[6,12288]{1,0:T(8,128)(2,1)S(1)}, bf16[6,12288]{1,0:T(8,128)(2,1)S(1)}, u32[]{:S(2)}, u32[]{:S(2)}) collective-permute-start(bf16[6,12288]{1,0:T(8,128)(2,1)S(1)} %slice.72), channel_id=1, source_target_pairs={{0,1},{1,2},{2,3},{3,4},{4,5},{5,6},{6,7},{7,8},{8,9},{9,10},{10,1... | collective-permute-start | bytes 442376 | tf_op jit(solution)/shard_map/ppermute | solution.py:14
  381.7 2.7 copy-start.4
  388.8 40.5 %all-to-all-start = ((f32[128,128,32]{0,2,1:T(8,128)}), f32[128,128,32]{0,2,1:T(8,128)}, u32[]{:S(2)}, u32[]{:S(2)}) async-start(f32[128,128,32]{0,2,1:T(8,128)} %bitcast.115), calls=%async_computation | async-start | bytes 4194304 | tf_op jit(solution)/shard_map/all_to_all | solution.py:112
  399.9 6.8 %copy-start.2 = (f32[256,128,32]{1,0,2:T(8,128)S(1)}, f32[256,128,32]{1,0,2:T(8,128)}, u32[]{:S(2)}) copy-start(f32[256,128,32]{1,0,2:T(8,128)} %fusion.38) | copy-start | bytes 12582916
  399.9 6.8 %copy-start.3 = (f32[256,128,32]{1,0,2:T(8,128)S(1)}, f32[256,128,32]{1,0,2:T(8,128)}, u32[]{:S(2)}) copy-start(f32[256,128,32]{1,0,2:T(8,128)} %fusion.40) | copy-start | bytes 12582916
  432.4 5.7 %copy-start.5 = (f32[128,128,32]{1,0,2:T(8,128)S(1)}, f32[128,128,32]{1,0,2:T(8,128)}, u32[]{:S(2)}) copy-start(f32[128,128,32]{1,0,2:T(8,128)} %copy.41) | copy-start | bytes 6291460
  510.7 38.6 %copy-start.8 = (f32[4096]{0:T(1024)S(1)}, f32[4096]{0:T(1024)}, u32[]{:S(2)}) copy-start(f32[4096]{0:T(1024)} %param.13) | copy-start | bytes 49156
  546.2 8.1 %copy-start.1 = (bf16[8192,96]{0,1:T(8,128)(2,1)S(1)}, bf16[8192,96]{0,1:T(8,128)(2,1)}, u32[]{:S(2)}) copy-start(bf16[8192,96]{0,1:T(8,128)(2,1)} %param.10) | copy-start | bytes 4718596
Sparse Core Ops, SparseCore 0:
  16.6 336.8 all-gather.1
where the time goes:
time: 571 us; the launch traced here: 562 us
  waiting for transfers between devices  319 us (56%)
  matrix products  129 us (23%)
  blocking collectives  35.6 us (6%)
  starting transfers between devices  26.6 us (5%)
  local copies, waits for them, and re-layouts  19.3 us (3%)
  other arithmetic  18.4 us (3%)
  between operations  14.1 us (2%)
    all_gather x1, waiting for transfers between devices, project_table(): return lax.all_gather(own_columns, ('row', 'col'), axis=1, tiled=True)  282 us
    dot_general x18, matrix products, contract(): jnp.einsum(form, table_part, data_part, precision=lax.Precision.HIGHEST)  116 us
    all_to_all x1, blocking collectives, local(): lax.all_to_all(causal_all, ('row', 'col'), split_axis=0, concat_axis=1, t...  35.6 us
    all_to_all x1, waiting for transfers between devices, local(): lax.all_to_all(long_filter, ('row', 'col'), split_axis=1, concat_axis=0,...  30.5 us
    all_to_all x1, starting transfers between devices, local(): lax.all_to_all(long_filter, ('row', 'col'), split_axis=1, concat_axis=0,...  11.7 us
  transfers between devices with their start and end apart: 4, of which 3 were waited for; matrix products, arithmetic and copies ran while one was open for 8% of the time, Pallas kernels for 0%

commit v1 on v0

--- a/solution.py
+++ b/solution.py
@@ -28,7 +28,12 @@
     inverse_rms = lax.rsqrt(jnp.mean(rows_f32 * rows_f32, axis=1, keepdims=True) + EPSILON)
     normed = (rows_f32 * inverse_rms * norm_gain.astype(jnp.float32)).astype(jnp.bfloat16)
     own_columns = jnp.dot(normed, w_in, preferred_element_type=jnp.float32).astype(jnp.bfloat16)
-    return lax.all_gather(own_columns, ("row", "col"), axis=1, tiled=True)
+    return jnp.concatenate(
+        lax.all_to_all(
+            jnp.stack([own_columns] * lax.axis_size(("row", "col"))), ("row", "col"), 0, 0
+        ),
+        axis=1,
+    )
 
 
 def short_filter(mixed_rows, short_taps):

time: 571 us -> 437 us (0.77)
  waiting for transfers between devices: 319 us -> 186 us
  between operations: 14.1 us -> 0.58 us
  starting transfers between devices: 26.6 us -> 38.2 us
    all_gather x1 -> x0, waiting for transfers between devices: 282 us -> none  [project_table(): return lax.all_gather(own_columns, ('row', 'col'), axis=1, tiled=True)]
    all_to_all x0 -> x1, waiting for transfers between devices: none -> 159 us  [project_table(): lax.all_to_all(jnp.stack([own_columns] * lax.axis_size(('row', 'col'))),...]
    all_to_all x1, waiting for transfers between devices: 30.5 us -> 20.6 us  [local(): lax.all_to_all(long_filter, ('row', 'col'), split_axis=1, concat_axis=0,...]
    all_to_all x0 -> x1, starting transfers between devices: none -> 6.25 us  [project_table(): lax.all_to_all(jnp.stack([own_columns] * lax.axis_size(('row', 'col'))),...]
    another operation x0 -> x1, local copies, waits for them, and re-layouts: none -> 6.06 us  [project_table(): jnp.stack([own_columns] * lax.axis_size(('row', 'col')))]
  transfers between devices with their start and end apart: 4 -> 4, of which waited for: 3 -> 3; matrix products, arithmetic and copies ran while one was open for 8% -> 12% of each run, Pallas kernels for 0% -> 0%
where the time goes in v1:
time: 437 us; the launch traced here: 431 us
  waiting for transfers between devices  186 us (43%)
  matrix products  128 us (29%)
  starting transfers between devices  38.2 us (9%)
  blocking collectives  35.6 us (8%)
  local copies, waits for them, and re-layouts  24.9 us (6%)
  other arithmetic  18.4 us (4%)
    all_to_all x1, waiting for transfers between devices, project_table(): lax.all_to_all(jnp.stack([own_columns] * lax.axis_size(('row', 'col'))),...  159 us
    dot_general x18, matrix products, contract(): jnp.einsum(form, table_part, data_part, precision=lax.Precision.HIGHEST)  116 us
    all_to_all x1, blocking collectives, local(): lax.all_to_all(causal_all, ('row', 'col'), split_axis=0, concat_axis=1, t...  35.6 us
    all_to_all x1, waiting for transfers between devices, local(): lax.all_to_all(long_filter, ('row', 'col'), split_axis=1, concat_axis=0,...  20.6 us
    all_to_all x1, starting transfers between devices, local(): lax.all_to_all(signal, ('row', 'col'), split_axis=1, concat_axis=0, tiled...  16 us
    all_to_all x1, starting transfers between devices, local(): lax.all_to_all(long_filter, ('row', 'col'), split_axis=1, concat_axis=0,...  11.7 us
    dot_general x1, matrix products, local(): jnp.dot(one_hot, lookup_table, preferred_element_type=jnp.float32)  8.76 us
  transfers between devices with their start and end apart: 4, of which 3 were waited for; matrix products, arithmetic and copies ran while one was open for 12% of the time, Pallas kernels for 0%

profile of v1, /device:TPU:0, one launch (start us, length us, event | category | flops | bytes accessed | tf_op | source)
XLA Modules:
  0.0 431.4 jit_solution(13385738157031892564)
XLA Ops:
  3.0 11.7 %all-to-all-start.2 = ((f32[128,128,32]{0,2,1:T(8,128)}), f32[128,128,32]{0,2,1:T(8,128)}, u32[]{:S(2)}, u32[]{:S(2)}) async-start(f32[128,128,32]{0,2,1:T(8,128)} %bitcast.118), calls=%async_computation.2 | async-start | bytes 4194304 | tf_op jit(solution)/shard_map/all_to_all | solution.py:118
  14.8 5.3 %fusion = f32[512]{0:T(512)S(1)} fusion(bf16[512,8192]{1,0:T(8,128)(2,1)} %param.8), kind=kLoop, calls=%fused_computation.2 | loop fusion | flops 12582400 | bytes 8390656 | tf_op jit(solution)/shard_map/reduce_sum | solution.py:28
  23.6 20.6 %all-to-all-done.2 = f32[128,128,32]{0,2,1:T(8,128)} async-done(((f32[128,128,32]{0,2,1:T(8,128)}), f32[128,128,32]{0,2,1:T(8,128)}, u32[]{:S(2)}, u32[]{:S(2)}) %all-to-all-start.2) | async-done | bytes 2097184 | tf_op jit(solution)/shard_map/all_to_all | solution.py:118
  44.1 6.1 %stack.2 = bf16[128,512,96]{1,2,0:T(8,128)(2,1)} broadcast(bf16[512,96]{0,1:T(8,128)(2,1)S(1)} %fusion.54), dimensions={1,2} | broadcast | bytes 12681216 | tf_op jit(solution)/shard_map/stack | solution.py:33
  50.2 6.2 %all-to-all-start = ((bf16[128,512,96]{1,2,0:T(8,128)(2,1)}), bf16[128,512,96]{1,2,0:T(8,128)(2,1)}, u32[]{:S(2)}, u32[]{:S(2)}) async-start(bf16[128,512,96]{1,2,0:T(8,128)(2,1)} %stack.2), calls=%async_computation | async-start | bytes 25165824 | tf_op jit(solution)/shard_map/all_to_all | solution.py:32
  57.5 9.4 %fusion.38 = f32[256,128,32]{1,0,2:T(8,128)} fusion(f32[128,128,32]{0,2,1:T(8,128)} %all-to-all-done.2), kind=kOutput, calls=%fused_computation.58 | convolution fusion | flops 1611071488 | bytes 6291456 | tf_op jit(solution)/shard_map/sk,sjc->ckj/dot_general | solution.py:23
  66.8 158.6 %all-to-all-done = bf16[128,512,96]{1,2,0:T(8,128)(2,1)} async-done(((bf16[128,512,96]{1,2,0:T(8,128)(2,1)}), bf16[128,512,96]{1,2,0:T(8,128)(2,1)}, u32[]{:S(2)}, u32[]{:S(2)}) %all-to-all-start) | async-done | bytes 12582944 | tf_op jit(solution)/shard_map/all_to_all | solution.py:32
  225.4 8.8 %convolution_convert_fusion = bf16[128,12288]{1,0:T(8,128)(2,1)S(1)} fusion(bf16[512,12288]{0,1:T(8,128)(2,1)} %bitcast.2, s32[128]{0:T(128)S(1)} %copy-done.10), kind=kOutput, calls=%fused_computation.5 | convolution fusion | flops 1612251136 | bytes 15729152 | tf_op jit(solution)/shard_map/dot_general | solution.py:109
  234.2 4.3 collective-permute-start
  238.5 9.4 %fusion.40 = f32[256,128,32]{1,0,2:T(8,128)} fusion(f32[128,128,32]{0,2,1:T(8,128)} %all-to-all-done.2), kind=kOutput, calls=%fused_computation.60 | convolution fusion | flops 1611071488 | bytes 6291456 | tf_op jit(solution)/shard_map/sk,sjc->ckj/dot_general | solution.py:23
  248.8 5.2 %fusion.7 = f32[128,12288]{1,0:T(8,128)S(1)} fusion(f32[134,12288]{1,0:T(8,128)S(1)} %maximum_convert_fusion, f32[12288]{0:T(1024)S(1)} %bitcast.125, f32[12288]{0:T(1024)S(1)} %bitcast.126, f32[12288]{0:T(1024)S(1)} %bitcast.121, f32[12288]{0:T(1024)S(1)} %bitcast.122, f32[12288]{0:T(1024)S(1)} %bitcast.123, f32[12288]{0:T(1024)S(1)} %bitcast.124, ...), kind=kLoop, calls=%fused_computation.10 | loop fusion | flops 20447232 | bytes 50675712 | tf_op jit(solution)/shard_map/add | solution.py:47
  261.1 16.0 %all-to-all-start.1 = ((f32[128,128,32]{0,2,1:T(8,128)}), f32[128,128,32]{0,2,1:T(8,128)}, u32[]{:S(2)}, u32[]{:S(2)}) async-start(f32[128,128,32]{0,2,1:T(8,128)} %bitcast.117), calls=%async_computation.1 | async-start | bytes 4194304 | tf_op jit(solution)/shard_map/all_to_all | solution.py:117
  277.1 6.8 %fusion.13 = f32[32,256,128]{2,1,0:T(8,128)S(1)} fusion(f32[256,128,32]{1,0,2:T(8,128)} %fusion.40, f32[256,128,32]{1,0,2:T(8,128)} %fusion.38, f32[256,128]{1,0:T(8,128)S(1)} %copy.50, f32[256,128]{1,0:T(8,128)S(1)} %copy.48), kind=kOutput, calls=%fused_computation.22 | convolution fusion | flops 1615036416 | bytes 12845056 | tf_op jit(solution)/shard_map/jm,ckj->ckm/dot_general | solution.py:23
  283.9 4.2 fusion.15
  288.2 5.8 %fusion.34 = f32[32,256,128]{2,1,0:T(8,128)} fusion(f32[32,256,128]{2,1,0:T(8,128)S(1)} %fusion.13, f32[256,128,32]{1,0,2:T(8,128)S(1)} %copy-done.3, f32[256,128,32]{1,0,2:T(8,128)S(1)} %copy-done.2, f32[256,128]{1,0:T(8,128)S(1)} %copy.50, f32[256,128]{1,0:T(8,128)S(1)} %copy.48), kind=kOutput, calls=%fused_computation.50 | convolution fusion | flops 1616084992 | bytes 17039360 | tf_op jit(solution)/shard_map/jm,ckj->ckm/dot_general | solution.py:23
  293.9 5.8 %fusion.31 = f32[32,256,128]{2,1,0:T(8,128)} fusion(f32[32,256,128]{2,1,0:T(8,128)S(1)} %fusion.15, f32[256,128,32]{1,0,2:T(8,128)S(1)} %copy-done.3, f32[256,128,32]{1,0,2:T(8,128)S(1)} %copy-done.2, f32[256,128]{1,0:T(8,128)S(1)} %copy.50, f32[256,128]{1,0:T(8,128)S(1)} %copy.48), kind=kOutput, calls=%fused_computation.49 | convolution fusion | flops 1616084992 | bytes 17039360 | tf_op jit(solution)/shard_map/jm,ckj->ckm/dot_general | solution.py:23
  299.7 6.8 %all-to-all-done.1 = f32[128,128,32]{0,2,1:T(8,128)} async-done(((f32[128,128,32]{0,2,1:T(8,128)}), f32[128,128,32]{0,2,1:T(8,128)}, u32[]{:S(2)}, u32[]{:S(2)}) %all-to-all-start.1) | async-done | bytes 2097184 | tf_op jit(solution)/shard_map/all_to_all | solution.py:117
  306.5 3.1 copy.42
  309.7 5.7 %fusion.42 = f32[128,32,256]{2,0,1:T(8,128)S(1)} fusion(f32[128,128,32]{1,0,2:T(8,128)} %copy.42), kind=kOutput, calls=%fused_computation.62 | convolution fusion | flops 1611071488 | bytes 6291456 | tf_op jit(solution)/shard_map/sk,sjc->ckj/dot_general | solution.py:23
  315.4 4.0 fusion.44
  319.4 9.5 %fusion.57 = f32[32,256,128]{2,1,0:T(8,128)} fusion(f32[128,32,256]{2,0,1:T(8,128)S(1)} %fusion.44, f32[128,32,256]{2,0,1:T(8,128)S(1)} %fusion.42, f32[256,128]{0,1:T(8,128)S(1)} %get-tuple-element.14, f32[256,128]{0,1:T(8,128)S(1)} %get-tuple-element.15), kind=kOutput, calls=%fused_computation.74 | convolution fusion | flops 1615036416 | bytes 12845056 | tf_op jit(solution)/shard_map/jm,ckj->ckm/dot_general | solution.py:23
  328.9 7.7 %fusion.61 = f32[32,256,128]{2,1,0:T(8,128)S(1)} fusion(f32[128,32,256]{2,0,1:T(8,128)S(1)} %fusion.44, f32[128,32,256]{2,0,1:T(8,128)S(1)} %fusion.42, f32[256,128]{0,1:T(8,128)S(1)} %get-tuple-element.14, f32[256,128]{0,1:T(8,128)S(1)} %get-tuple-element.15), kind=kOutput, calls=%fused_computation.75 | convolution fusion | flops 1615036416 | bytes 12845056 | tf_op jit(solution)/shard_map/jm,ckj->ckm/dot_general | solution.py:23
  336.6 9.1 %convolution_add_fusion.1 = f32[32,256,128]{2,1,0:T(8,128)} fusion(f32[32,256,128]{2,1,0:T(8,128)S(1)} %fusion.61, f32[128,32,256]{2,0,1:T(8,128)S(1)} %fusion.44, f32[128,32,256]{2,0,1:T(8,128)S(1)} %fusion.42, f32[256,128]{0,1:T(8,128)S(1)} %get-tuple-element.14, f32[256,128]{0,1:T(8,128)S(1)} %get-tuple-element.15), kind=kOutput, calls=%fused_computation.54 | convolution fusion | flops 1616084992 | bytes 17039360 | tf_op jit(solution)/shard_map/jm,ckj->ckm/dot_general | solution.py:23
  345.7 11.9 %multiply_add_fusion = (f32[32,256,128]{2,1,0:T(8,128)S(1)}, f32[32,256,128]{2,1,0:T(8,128)S(1)}) fusion(f32[32,256,128]{2,1,0:T(8,128)} %fusion.31, f32[32,256,128]{2,1,0:T(8,128)} %convolution_add_fusion.1, f32[32,256,128]{2,1,0:T(8,128)} %fusion.34, f32[32,256,128]{2,1,0:T(8,128)} %fusion.57, f32[128,32,256]{2,0,1:T(8,128)S(1)} %fusion.44, ...), kind=kOutput, calls=%fused_computation.44 | convolution fusion | flops 1622376448 | bytes 33816576 | tf_op jit(solution)/shard_map/jm,ckj->ckm/dot_general | solution.py:23
  357.6 4.2 fusion.91
  361.8 4.2 fusion.93
  366.0 4.5 %convolution_add_fusion = f32[32,256,128]{1,2,0:T(8,128)S(1)} fusion(f32[32,256,128]{1,2,0:T(8,128)S(1)} %fusion.91, f32[32,256,128]{2,1,0:T(8,128)S(1)} %get-tuple-element.6), kind=kOutput, calls=%fused_computation.51 | convolution fusion | flops 1611890688 | bytes 12582912 | tf_op jit(solution)/shard_map/jm,ckm->ckj/dot_general | solution.py:23
  370.4 4.2 convolution_subtract_fusion
  374.7 4.0 fusion.23
  378.7 5.7 %multiply_bitcast_fusion = f32[128,128,32]{0,1,2:T(8,128)} fusion(f32[32,128,128]{2,1,0:T(8,128)S(1)} %fusion.23, f32[32,256,128]{1,2,0:T(8,128)S(1)} %convolution_add_fusion, f32[32,256,128]{1,2,0:T(8,128)S(1)} %convolution_subtract_fusion, f32[256,128]{0,1:T(8,128)S(1)} %get-tuple-element.14, f32[256,128]{0,1:T(8,128)S(1)} %get-tuple-element.15), kind=kOutput, calls=%fused_computation.66 | convolution fusion | flops 1615265792 | bytes 12845056 | tf_op jit(solution)/shard_map/sk,ckj->sjc/dot_general | solution.py:23
  387.6 35.6 %all_to_all.53 = f32[128,128,32]{1,2,0:T(8,128)} all-to-all(f32[128,128,32]{1,2,0:T(8,128)} %copy.57), channel_id=1, replica_groups=mesh['row'=16,'col'=8] {'row','col'}, dimensions={0} | all-to-all | bytes 4194304 | tf_op jit(solution)/shard_map/all_to_all | solution.py:121
  426.1 5.0 %fusion.37 = bf16[128,4096]{1,0:T(8,128)(2,1)} fusion(f32[128,12288]{1,0:T(8,128)} %copy-done.4, f32[128,4096]{1,0:T(8,128)} %copy.58, f32[4096]{0:T(1024)S(1)} %copy-done.8), kind=kLoop, calls=%fused_computation.57 | loop fusion | flops 2621440 | bytes 9453568 | tf_op jit(solution)/shard_map/convert_element_type | solution.py:123
  (37 shorter events, 21.8 us)
Async XLA Ops:
  0.0 20.0 %copy-start = (bf16[8192,96]{0,1:T(8,128)(2,1)S(1)}, bf16[8192,96]{0,1:T(8,128)(2,1)}, u32[]{:S(2)}) copy-start(bf16[8192,96]{0,1:T(8,128)(2,1)} %param.10) | copy-start | bytes 4718596
  0.0 14.7 %copy-start.9 = (bf16[8192]{0:T(1024)(128)(2,1)S(1)}, bf16[8192]{0:T(1024)(128)(2,1)}, u32[]{:S(2)}) copy-start(bf16[8192]{0:T(1024)(128)(2,1)} %param.9) | copy-start | bytes 49156
  3.0 41.1 %all-to-all-start.2 = ((f32[128,128,32]{0,2,1:T(8,128)}), f32[128,128,32]{0,2,1:T(8,128)}, u32[]{:S(2)}, u32[]{:S(2)}) async-start(f32[128,128,32]{0,2,1:T(8,128)} %bitcast.118), calls=%async_computation.2 | async-start | bytes 4194304 | tf_op jit(solution)/shard_map/all_to_all | solution.py:118
  14.7 5.8 %copy-start.6 = (bf16[512,8192]{1,0:T(8,128)(2,1)S(1)}, bf16[512,8192]{1,0:T(8,128)(2,1)}, u32[]{:S(2)}) copy-start(bf16[512,8192]{1,0:T(8,128)(2,1)} %param.8) | copy-start | bytes 25165828
  50.2 7.0 %copy-start.7 = (f32[7,12288]{1,0:T(8,128)S(1)}, f32[7,12288]{1,0:T(8,128)}, u32[]{:S(2)}) copy-start(f32[7,12288]{1,0:T(8,128)} %param.11) | copy-start | bytes 1032196
  50.2 175.2 %all-to-all-start = ((bf16[128,512,96]{1,2,0:T(8,128)(2,1)}), bf16[128,512,96]{1,2,0:T(8,128)(2,1)}, u32[]{:S(2)}, u32[]{:S(2)}) async-start(bf16[128,512,96]{1,2,0:T(8,128)(2,1)} %stack.2), calls=%async_computation | async-start | bytes 25165824 | tf_op jit(solution)/shard_map/all_to_all | solution.py:32
  56.5 169.0 %copy-start.10 = (s32[128]{0:T(128)S(1)}, s32[128]{0:T(128)}, u32[]{:S(2)}) copy-start(s32[128]{0:T(128)} %param.7) | copy-start | bytes 1540
  234.2 13.7 %collective-permute-start = (bf16[6,12288]{1,0:T(8,128)(2,1)S(1)}, bf16[6,12288]{1,0:T(8,128)(2,1)S(1)}, u32[]{:S(2)}, u32[]{:S(2)}) collective-permute-start(bf16[6,12288]{1,0:T(8,128)(2,1)S(1)} %slice.72), channel_id=1, source_target_pairs={{0,1},{1,2},{2,3},{3,4},{4,5},{5,6},{6,7},{7,8},{8,9},{9,10},{10,1... | collective-permute-start | bytes 442376 | tf_op jit(solution)/shard_map/ppermute | solution.py:14
  254.0 2.7 copy-start.4
  261.1 45.4 %all-to-all-start.1 = ((f32[128,128,32]{0,2,1:T(8,128)}), f32[128,128,32]{0,2,1:T(8,128)}, u32[]{:S(2)}, u32[]{:S(2)}) async-start(f32[128,128,32]{0,2,1:T(8,128)} %bitcast.117), calls=%async_computation.1 | async-start | bytes 4194304 | tf_op jit(solution)/shard_map/all_to_all | solution.py:117
  277.1 6.8 %copy-start.2 = (f32[256,128,32]{1,0,2:T(8,128)S(1)}, f32[256,128,32]{1,0,2:T(8,128)}, u32[]{:S(2)}) copy-start(f32[256,128,32]{1,0,2:T(8,128)} %fusion.38) | copy-start | bytes 12582916
  277.1 6.8 %copy-start.3 = (f32[256,128,32]{1,0,2:T(8,128)S(1)}, f32[256,128,32]{1,0,2:T(8,128)}, u32[]{:S(2)}) copy-start(f32[256,128,32]{1,0,2:T(8,128)} %fusion.40) | copy-start | bytes 12582916
  309.7 5.7 %copy-start.5 = (f32[128,128,32]{1,0,2:T(8,128)S(1)}, f32[128,128,32]{1,0,2:T(8,128)}, u32[]{:S(2)}) copy-start(f32[128,128,32]{1,0,2:T(8,128)} %copy.42) | copy-start | bytes 6291460
  387.6 38.6 %copy-start.8 = (f32[4096]{0:T(1024)S(1)}, f32[4096]{0:T(1024)}, u32[]{:S(2)}) copy-start(f32[4096]{0:T(1024)} %param.13) | copy-start | bytes 49156
  423.1 8.0 %copy-start.1 = (bf16[8192,96]{0,1:T(8,128)(2,1)S(1)}, bf16[8192,96]{0,1:T(8,128)(2,1)}, u32[]{:S(2)}) copy-start(bf16[8192,96]{0,1:T(8,128)(2,1)} %param.10) | copy-start | bytes 4718596
